TPU v7x, 128 devices: a whole 4x4x4 slice. The times are simulated.
128 devices in a mesh: expert: 4 (over z), dp: 32 (over x, y, core).
Axes of the slice: x: 4, y: 4, z: 4, core: 2. Of those that a mesh axis runs over, the one named last changes fastest.
Arguments:
- tokens: bfloat16 [65536, 512], P(('expert', 'dp')), may hold values from -6 to 6
- segments: int32 [128, 512], P(('expert', 'dp')), may hold values from 0 to 31, never falling along the last dimension, each value on 1 to 49 neighbouring positions
- routes: int32 [65536, 2], P(('expert', 'dp')), may hold values from 0 to 31, all different within a row; in each aligned block of 512 rows (0 to 511, 512 to 1023, ...) at most 64 rows name the same one
- priority: int32 [65536], P(('expert', 'dp')), may hold values from 0 to 65535, each once
- ln1_gain: float32 [512], replicated, may hold values from 0.1 to 1.9
- ln1_bias: float32 [512], replicated, may hold values from -3 to 3
- w_qkv: bfloat16 [512, 1536], replicated, may hold values from -0.25 to 0.25
- w_out: bfloat16 [512, 512], replicated, may hold values from -1 to 1
- ln2_gain: float32 [512], replicated, may hold values from 0.1 to 1.9
- ln2_bias: float32 [512], replicated, may hold values from -3 to 3
- w_router: bfloat16 [512, 32], replicated, may hold values from -0.1875 to 0.1875
- expert_in: bfloat16 [32, 512, 2048], P('dp', None, 'expert'), may hold values from -0.25 to 0.25
- expert_out: bfloat16 [32, 2048, 512], P('dp', 'expert'), may hold values from -2 to 2
- cotangent: bfloat16 [65536, 512], P(('expert', 'dp')), may hold values from -6 to 6
Outputs:
- output: bfloat16 [65536, 512], P(('expert', 'dp'))
- d_tokens: float32 [65536, 512], P(('expert', 'dp'))
- d_ln1_gain: float32 [512], replicated
- d_ln1_bias: float32 [512], replicated
- d_w_qkv: float32 [512, 1536], replicated
- d_w_out: float32 [512, 512], replicated
- d_ln2_gain: float32 [512], replicated
- d_ln2_bias: float32 [512], replicated
- d_w_router: float32 [512, 32], replicated
- d_expert_in: float32 [32, 512, 2048], P('dp', None, 'expert')
- d_expert_out: float32 [32, 2048, 512], P('dp', 'expert')
Inputs may be any that keep to these rules, and one draw needn't show every extreme that they name: `routes`: of the rows of one device, each expert is named by at most 64, a bound that some block reaches. `segments`: ids never fall along a row; each id covers 1 to 49 slots, some exactly 49. `priority`: A permutation.
All inputs are finite; a program needn't handle non-finite values.
Results may differ from a plain program's by a relative error of at most 0.018.
Values may be sent and summed in bfloat16 or wider, within the bound.
No kernel may reach another device: no remote copies, remote signals or barrier semaphores. Data moves between devices by JAX's collectives and lax.ppermute only.
A program may use at most 192 MiB of HBM per device.

v0:
```python
import jax
import jax.numpy as jnp
from jax import lax
from jax.sharding import PartitionSpec as P

D = 512
HEADS = 8
HDIM = 64
EXPERTS = 32
MOST = 64


eps_norm = 1e-06


def norm_forward(values, gain_vec, shift_vec):
    center = values - jnp.mean(values, axis=-1, keepdims=True)
    factor = lax.rsqrt(jnp.mean(center * center, axis=-1, keepdims=True) + eps_norm)
    normal = center * factor
    return (normal * gain_vec + shift_vec, normal, factor)


def norm_backward(upstream, normal, factor, gain_vec):
    scaled = upstream * gain_vec
    inner_term = (
        scaled
        - jnp.mean(scaled, axis=-1, keepdims=True)
        - normal * jnp.mean(scaled * normal, axis=-1, keepdims=True)
    )
    return (inner_term * factor, jnp.sum(upstream * normal, axis=0), jnp.sum(upstream, axis=0))


def gelu_tanh(values):
    return jax.nn.gelu(values, approximate=True)


def split_heads(packed):
    heads_view = packed.reshape(packed.shape[0], 3, HEADS, HDIM)
    return (heads_view[:, 0], heads_view[:, 1], heads_view[:, 2])


def score_table(queries, keys_in, labels):
    same_doc = labels[:, None] == labels[None, :]
    scores = jnp.einsum(
        "qhc,khc->hqk", queries, keys_in, preferred_element_type=jnp.float32
    ) * HDIM ** (-0.5)
    return jnp.where(same_doc[None], scores, -1e30)


def attend_forward(packed, labels):
    queries, keys_in, values = split_heads(packed)
    scores = score_table(queries, keys_in, labels)
    highest = jnp.max(scores, axis=-1, keepdims=True)
    raised = jnp.exp(scores - highest)
    totals = jnp.sum(raised, axis=-1, keepdims=True)
    weights = (raised / totals).astype(jnp.bfloat16)
    attended = jnp.einsum("hqk,khc->qhc", weights, values, preferred_element_type=jnp.float32)
    return (attended, highest + jnp.log(totals))


def attend_backward(packed, labels, logsum, upstream):
    queries, keys_in, values = split_heads(packed)
    weights = jnp.exp(score_table(queries, keys_in, labels) - logsum)
    d_values = jnp.einsum(
        "hqk,qhc->khc", weights.astype(jnp.bfloat16), upstream, preferred_element_type=jnp.float32
    )
    d_weights = jnp.einsum("qhc,khc->hqk", upstream, values, preferred_element_type=jnp.float32)
    row_inner = jnp.sum(weights * d_weights, axis=-1, keepdims=True)
    d_scores = (weights * (d_weights - row_inner)).astype(jnp.bfloat16)
    d_queries = jnp.einsum(
        "hqk,khc->qhc", d_scores, keys_in, preferred_element_type=jnp.float32
    ) * HDIM ** (-0.5)
    d_keys = jnp.einsum(
        "hqk,qhc->khc", d_scores, queries, preferred_element_type=jnp.float32
    ) * HDIM ** (-0.5)
    stacked = jnp.stack([d_queries, d_keys, d_values], axis=1).astype(jnp.bfloat16)
    return stacked.reshape(stacked.shape[0], 3 * HEADS * HDIM)


def to_expert_layout(arrived, local_count):
    source_count = arrived.shape[0] // local_count
    shaped = arrived.reshape((source_count, local_count) + arrived.shape[1:])
    shaped = jnp.swapaxes(shaped, 0, 1)
    return shaped.reshape((local_count, source_count * arrived.shape[1]) + arrived.shape[2:])


def to_source_layout(partial_value, local_count):
    source_count = partial_value.shape[1] // MOST
    shaped = partial_value.reshape((local_count, source_count, MOST) + partial_value.shape[2:])
    shaped = jnp.swapaxes(shaped, 0, 1)
    return shaped.reshape((source_count * local_count, MOST) + partial_value.shape[2:])


def per_device(
    tokens,
    segments,
    routes,
    priority,
    ln1_gain,
    ln1_bias,
    w_qkv,
    w_out,
    ln2_gain,
    ln2_bias,
    w_router,
    expert_in,
    expert_out,
    cotangent,
):
    row_count = tokens.shape[0]
    column_size = lax.axis_size("expert")
    tokens_all = row_count * column_size * lax.axis_size("dp")
    capacity = (21 * tokens_all + 319) // 320
    sentinel = 2 * tokens_all
    local_count = expert_in.shape[0]
    labels = segments[0]
    inputs = tokens.astype(jnp.float32)
    normed1, normal1, factor1 = norm_forward(inputs, ln1_gain, ln1_bias)
    first_low = normed1.astype(jnp.bfloat16)
    packed = jnp.dot(first_low, w_qkv, preferred_element_type=jnp.float32).astype(jnp.bfloat16)
    attended, logsum = attend_forward(packed, labels)
    attended_low = attended.astype(jnp.bfloat16).reshape(row_count, D)
    residual = inputs + jnp.dot(attended_low, w_out, preferred_element_type=jnp.float32)
    normed2, normal2, factor2 = norm_forward(residual, ln2_gain, ln2_bias)
    second_low = normed2.astype(jnp.bfloat16)
    logits = jnp.dot(second_low, w_router, preferred_element_type=jnp.float32)
    raised = jnp.exp(logits - jnp.max(logits, axis=-1, keepdims=True))
    router_prob = raised / jnp.sum(raised, axis=-1, keepdims=True)
    gate_pick = jnp.take_along_axis(router_prob, routes, axis=1)
    flat_route = routes.reshape(-1)
    expert_iota = jnp.arange(EXPERTS, dtype=jnp.int32)
    onehot = (flat_route[:, None] == expert_iota[None, :]).astype(jnp.int32)
    within = jnp.sum((jnp.cumsum(onehot, axis=0) - onehot) * onehot, axis=1)
    position = flat_route * MOST + within
    slot_iota = jnp.arange(2 * row_count, dtype=jnp.int32)
    matches = position[None, :] == jnp.arange(EXPERTS * MOST, dtype=jnp.int32)[:, None]
    source = jnp.sum(jnp.where(matches, slot_iota[None, :] + 1, 0), axis=1) - 1
    filled = source >= 0
    source = jnp.maximum(source, 0)
    token_of = source // 2
    send_rows = jnp.where(
        filled[:, None], second_low[token_of], jnp.zeros((), jnp.bfloat16)
    ).reshape(EXPERTS, MOST, D)
    send_keys = jnp.where(filled, source % 2 * tokens_all + priority[token_of], sentinel).reshape(
        EXPERTS, MOST
    )
    moved_rows, moved_keys = (
        lax.all_to_all(send_rows, "dp", split_axis=0, concat_axis=0, tiled=True),
        lax.all_to_all(send_keys, "dp", split_axis=0, concat_axis=0, tiled=True),
    )
    recv_rows, recv_keys = (
        lax.all_gather(moved_rows, "expert", axis=0, tiled=True),
        lax.all_gather(moved_keys, "expert", axis=0, tiled=True),
    )
    expert_rows = to_expert_layout(recv_rows, local_count)
    expert_keys = to_expert_layout(recv_keys, local_count)
    first_full, second_full = (expert_in, expert_out)
    cutoff = -lax.top_k(-expert_keys, capacity)[0][:, capacity - 1 :]
    keep_mask = (expert_keys <= cutoff) & (expert_keys < sentinel)
    pre_act = jnp.einsum(
        "lrd,ldf->lrf", expert_rows, first_full, preferred_element_type=jnp.float32
    )
    activated = gelu_tanh(pre_act).astype(jnp.bfloat16)
    partial_out = jnp.einsum(
        "lrf,lfd->lrd", activated, second_full, preferred_element_type=jnp.float32
    )
    partial_out = jnp.where(keep_mask[:, :, None], partial_out, 0.0)
    outgoing = to_source_layout(partial_out, local_count)
    reduced = lax.psum_scatter(
        outgoing.astype(jnp.bfloat16), "expert", scatter_dimension=0, tiled=True
    )
    combined = lax.all_to_all(reduced, "dp", split_axis=0, concat_axis=0, tiled=True)
    slot_out = (
        combined.reshape(EXPERTS * MOST, D)[position].astype(jnp.float32).reshape(row_count, 2, D)
    )
    output = (residual + jnp.sum(gate_pick[:, :, None] * slot_out, axis=1)).astype(jnp.bfloat16)
    grad_out = cotangent.astype(jnp.float32)
    slot_grad = (
        (gate_pick[:, :, None] * grad_out[:, None, :])
        .astype(jnp.bfloat16)
        .reshape(2 * row_count, D)
    )
    gate_grad = jnp.sum(slot_out * grad_out[:, None, :], axis=2)
    send_grad = jnp.where(filled[:, None], slot_grad[source], jnp.zeros((), jnp.bfloat16)).reshape(
        EXPERTS, MOST, D
    )
    moved_grad = lax.all_to_all(send_grad, "dp", split_axis=0, concat_axis=0, tiled=True)
    recv_grad = lax.all_gather(moved_grad, "expert", axis=0, tiled=True)
    grad_rows = jnp.where(
        keep_mask[:, :, None], to_expert_layout(recv_grad, local_count), jnp.zeros((), jnp.bfloat16)
    )
    d_activated = jnp.einsum(
        "lrd,lfd->lrf", grad_rows, second_full, preferred_element_type=jnp.float32
    )
    again_pre = jnp.einsum(
        "lrd,ldf->lrf", expert_rows, first_full, preferred_element_type=jnp.float32
    )
    again_act = gelu_tanh(again_pre).astype(jnp.bfloat16)
    d_pre = jax.vjp(gelu_tanh, again_pre)[1](d_activated)[0].astype(jnp.bfloat16)
    d_expert_out = jnp.einsum(
        "lrf,lrd->lfd", again_act, grad_rows, preferred_element_type=jnp.float32
    )
    d_expert_in = jnp.einsum("lrd,lrf->ldf", expert_rows, d_pre, preferred_element_type=jnp.float32)
    d_partial = jnp.einsum("lrf,ldf->lrd", d_pre, first_full, preferred_element_type=jnp.float32)
    grad_outgoing = to_source_layout(d_partial, local_count)
    grad_reduced = lax.psum_scatter(
        grad_outgoing.astype(jnp.bfloat16), "expert", scatter_dimension=0, tiled=True
    )
    d_combined = lax.all_to_all(grad_reduced, "dp", split_axis=0, concat_axis=0, tiled=True)
    d_slots = (
        d_combined.reshape(EXPERTS * MOST, D)[position].astype(jnp.float32).reshape(row_count, 2, D)
    )
    route_hot = (routes[:, :, None] == expert_iota[None, None, :]).astype(jnp.float32)
    d_prob = jnp.sum(gate_grad[:, :, None] * route_hot, axis=1)
    d_logits = router_prob * (d_prob - jnp.sum(d_prob * router_prob, axis=-1, keepdims=True))
    router_full = w_router.astype(jnp.float32)
    d_router = jnp.einsum(
        "td,te->de", second_low.astype(jnp.float32), d_logits, precision=lax.Precision.HIGHEST
    )
    d_second = jnp.sum(d_slots, axis=1) + jnp.einsum(
        "te,de->td", d_logits, router_full, precision=lax.Precision.HIGHEST
    )
    d_norm2, d_gain2, d_shift2 = norm_backward(d_second, normal2, factor2, ln2_gain)
    d_residual = grad_out + d_norm2
    d_branch = d_residual.astype(jnp.bfloat16)
    d_w_out = jnp.einsum("td,te->de", attended_low, d_branch, preferred_element_type=jnp.float32)
    d_attended = jnp.einsum(
        "te,de->td", d_branch, w_out, preferred_element_type=jnp.float32
    ).astype(jnp.bfloat16)
    d_packed = attend_backward(packed, labels, logsum, d_attended.reshape(row_count, HEADS, HDIM))
    d_w_qkv = jnp.einsum("td,te->de", first_low, d_packed, preferred_element_type=jnp.float32)
    d_first = jnp.einsum("te,de->td", d_packed, w_qkv, preferred_element_type=jnp.float32)
    d_norm1, d_gain1, d_shift1 = norm_backward(d_first, normal1, factor1, ln1_gain)
    d_tokens = d_residual + d_norm1
    summed = lax.psum(
        (d_gain1, d_shift1, d_w_qkv, d_w_out, d_gain2, d_shift2, d_router), ("expert", "dp")
    )
    return (
        output,
        d_tokens,
        summed[0],
        summed[1],
        summed[2],
        summed[3],
        summed[4],
        summed[5],
        summed[6],
        d_expert_in,
        d_expert_out,
    )


def solution(mesh):
    in_specs = (
        P(("expert", "dp"), None),
        P(("expert", "dp"), None),
        P(("expert", "dp"), None),
        P(("expert", "dp")),
        P(),
        P(),
        P(),
        P(),
        P(),
        P(),
        P(),
        P("dp", None, "expert"),
        P("dp", "expert", None),
        P(("expert", "dp"), None),
    )
    out_specs = (
        P(("expert", "dp"), None),
        P(("expert", "dp"), None),
        P(),
        P(),
        P(),
        P(),
        P(),
        P(),
        P(),
        P("dp", None, "expert"),
        P("dp", "expert", None),
    )
    return jax.shard_map(
        per_device, mesh=mesh, in_specs=in_specs, out_specs=out_specs, check_vma=False
    )
```

profile of v0, /device:TPU:1, one launch (start us, length us, event | category | flops | bytes accessed | tf_op | source)
XLA Modules:
  0.0 750.5 jit_solution(17914211551776724697)
XLA Ops:
  9.4 9.0 %reduce-window.6 = s32[32,8,128]{2,1,0:T(8,128)S(1)} reduce-window(s32[32,8,128]{2,1,0:T(8,128)S(1)} %fusion.60, s32[]{:T(128)} %constant.84.clone.1), window={size=1x1x128 pad=0_0x0_0x127_0}, to_apply=%region_8.9 | reduce-window | flops 4161536 | bytes 262148 | tf_op jit(solution)/shard_map/reduce-window
  20.1 11.1 %gather_fusion = s32[2048]{0:T(1024)S(1)} fusion(s32[512]{0:T(512)} %param.17, s32[2048]{0:T(1024)S(1)} %broadcast_clamp_fusion), kind=kCustom, calls=%fused_computation | custom fusion | bytes 24576 | tf_op jit(solution)/shard_map/gather | solution.py:144
  32.0 8.9 %all-to-all-start = ((s32[32,1,64]{2,1,0:T(1,128)}), s32[32,1,64]{2,1,0:T(1,128)S(1)}, u32[]{:S(2)}, u32[]{:S(2)}) async-start(s32[32,1,64]{2,1,0:T(1,128)} %bitcast.12), calls=%async_computation | async-start | bytes 32768 | tf_op jit(solution)/shard_map/all_to_all | solution.py:149
  65.2 8.6 %gather_fusion.5 = f32[1024]{0:T(1024)S(1)} fusion(f32[512,32]{0,1:T(8,128)S(1)} %fusion.61, s32[1024]{0:T(1024)S(1)} %reshape.564), kind=kCustom, calls=%fused_computation.5 | custom fusion | bytes 16384 | tf_op jit(solution)/shard_map/jit(take_along_axis)/gather | solution.py:129
  74.5 9.2 %gather_fusion.1 = bf16[2048,512]{1,0:T(8,128)(2,1)} fusion(bf16[512,512]{1,0:T(8,128)(2,1)S(1)} %copy.201, s32[2048]{0:T(1024)S(1)} %broadcast_clamp_fusion), kind=kCustom, calls=%fused_computation.1 | custom fusion | bytes 4202496 | tf_op jit(solution)/shard_map/gather | solution.py:142
  85.5 9.2 %gather_fusion.3 = bf16[2048,512]{1,0:T(8,128)(2,1)} fusion(bf16[1024,512]{1,0:T(8,128)(2,1)S(1)} %multiply_convert_fusion.2, s32[2048]{0:T(1024)S(1)} %get-tuple-element.106), kind=kCustom, calls=%fused_computation.3 | custom fusion | bytes 4202496 | tf_op jit(solution)/shard_map/gather | solution.py:184
  98.5 7.6 %all-to-all-start.3 = ((bf16[32,64,512]{2,1,0:T(8,128)(2,1)}), bf16[32,64,512]{2,1,0:T(8,128)(2,1)}, u32[]{:S(2)}, u32[]{:S(2)}) async-start(bf16[32,64,512]{2,1,0:T(8,128)(2,1)} %get-tuple-element.111), calls=%async_computation.4 | async-start | bytes 4194304 | tf_op jit(solution)/shard_map/all_to_all | solution.py:187
  106.2 11.4 %all-gather = s32[128,1,64]{2,1,0:T(1,128)S(1)} all-gather(s32[32,1,64]{2,1,0:T(1,128)S(1)} %all-to-all-done), channel_id=2, replica_groups=mesh['expert'=4,'dp'=32] {'expert'}, dimensions={0}, use_global_device_ids=true | all-gather | bytes 40960 | tf_op jit(solution)/shard_map/all_gather | solution.py:153
  118.5 15.9 %all-to-all-done.3 = bf16[32,64,512]{2,1,0:T(8,128)(2,1)} async-done(((bf16[32,64,512]{2,1,0:T(8,128)(2,1)}), bf16[32,64,512]{2,1,0:T(8,128)(2,1)}, u32[]{:S(2)}, u32[]{:S(2)}) %all-to-all-start.3) | async-done | bytes 2097184 | tf_op jit(solution)/shard_map/all_to_all | solution.py:187
  134.5 33.5 %all_to_all.29 = bf16[32,64,512]{2,1,0:T(8,128)(2,1)} all-to-all(bf16[32,64,512]{2,1,0:T(8,128)(2,1)} %get-tuple-element.112), channel_id=1, replica_groups=mesh['expert'=4,'dp'=32] {'dp'}, dimensions={0} | all-to-all | bytes 4194304 | tf_op jit(solution)/shard_map/all_to_all | solution.py:148
  170.4 45.7 %all-gather.6.cloned.1.call-done = bf16[128,64,512]{2,1,0:T(8,128)(2,1)} async-done(((bf16[32,64,512]{2,1,0:T(8,128)(2,1)}), bf16[128,64,512]{2,1,0:T(8,128)(2,1)}) %all-gather.6.cloned.1.call-update) | async-done | bytes 8388624 | tf_op jit(solution)/shard_map/all_gather | solution.py:188
  216.1 10.4 %fusion.7 = f32[8192,512]{1,0:T(8,128)} fusion(bf16[1,8192,1,1,1,1,512]{6,1,5,4,3,2,0:T(8,128)(2,1)} %bitcast.125, pred[8192]{0:T(1024)(128)(4,1)S(1)} %and.60, bf16[1,512,512]{2,1,0:T(8,128)(2,1)S(1)} %copy-done.44), kind=kOutput, calls=%fused_computation.18 | convolution fusion | flops 4299161600 | bytes 25698304 | tf_op jit(solution)/shard_map/lrd,lfd->lrf/dot_general | solution.py:192
  226.5 75.2 %all-gather.4.cloned.1.call-done = bf16[128,64,512]{2,1,0:T(8,128)(2,1)} async-done(((bf16[32,64,512]{2,1,0:T(8,128)(2,1)}), bf16[128,64,512]{2,1,0:T(8,128)(2,1)}) %all-gather.4.cloned.1.call-update) | async-done | bytes 8388624 | tf_op jit(solution)/shard_map/all_gather | solution.py:152
  301.7 20.8 %fusion.6 = (bf16[8192,512]{1,0:T(8,128)(2,1)S(1)}, f32[8192,512]{1,0:T(8,128)}) fusion(f32[8192,512]{1,0:T(8,128)} %fusion.7, bf16[8192,512]{1,0:T(8,128)(2,1)} %bitcast.139, bf16[1,512,512]{2,1,0:T(8,128)(2,1)S(1)} %copy-done.43), kind=kOutput, calls=%fused_computation.14 | convolution fusion | flops 4378853376 | bytes 50855936 | tf_op jit(solution)/shard_map/lrd,ldf->lrf/dot_general | solution.py:160
  325.7 8.0 %fusion.14 = bf16[128,64,512]{2,0,1:T(8,128)(2,1)} fusion(bf16[128,64,512]{2,1,0:T(8,128)(2,1)S(1)} %bitcast.141, bf16[1,512,512]{2,1,0:T(8,128)(2,1)S(1)} %copy-done.43), kind=kOutput, calls=%fused_computation.33 | convolution fusion | flops 4299161600 | bytes 17301504 | tf_op jit(solution)/shard_map/lrf,ldf->lrd/dot_general | solution.py:204
  334.0 13.0 %select_convert_fusion = bf16[8192,512]{1,0:T(8,128)(2,1)} fusion(pred[8192]{0:T(1024)(128)(4,1)S(1)} %and.60, bf16[1,512,512]{2,1,0:T(8,128)(2,1)S(1)} %copy-done.44, f32[8192,512]{1,0:T(8,128)} %get-tuple-element.120), kind=kOutput, calls=%fused_computation.15 | convolution fusion | flops 4341104640 | bytes 25698304 | tf_op jit(solution)/shard_map/lrf,lfd->lrd/dot_general | solution.py:164
  347.7 67.7 %reduce-scatter.5.cloned.1.call-done = bf16[32,64,512]{2,0,1:T(8,128)(2,1)} async-done(((bf16[128,64,512]{2,0,1:T(8,128)(2,1)}), bf16[32,64,512]{2,0,1:T(8,128)(2,1)}) %reduce-scatter.5.cloned.1.call-update) | async-done | bytes 2097168 | tf_op jit(solution)/shard_map/reduce_scatter | solution.py:206
  419.5 7.6 %all-to-all-start.4 = ((bf16[32,64,512]{2,1,0:T(8,128)(2,1)}), bf16[32,64,512]{2,1,0:T(8,128)(2,1)}, u32[]{:S(2)}, u32[]{:S(2)}) async-start(bf16[32,64,512]{2,1,0:T(8,128)(2,1)} %copy.208), calls=%async_computation.6 | async-start | bytes 4194304 | tf_op jit(solution)/shard_map/all_to_all | solution.py:209
  434.6 63.5 %reduce-scatter.3.cloned.1.call-done = bf16[32,64,512]{2,1,0:T(8,128)(2,1)} async-done(((bf16[128,64,512]{2,1,0:T(8,128)(2,1)}), bf16[32,64,512]{2,1,0:T(8,128)(2,1)}) %reduce-scatter.3.cloned.1.call-update) | async-done | bytes 2097168 | tf_op jit(solution)/shard_map/reduce_scatter | solution.py:169
  498.1 7.6 %all-to-all-start.2 = ((bf16[32,64,512]{2,1,0:T(8,128)(2,1)}), bf16[32,64,512]{2,1,0:T(8,128)(2,1)}, u32[]{:S(2)}, u32[]{:S(2)}) async-start(bf16[32,64,512]{2,1,0:T(8,128)(2,1)} %reduce-scatter.3.cloned.1.call-done), calls=%async_computation.3 | async-start | bytes 4194304 | tf_op jit(solution)/shard_map/all_to_all | solution.py:172
  505.8 12.9 %convolution_bitcast_fusion = f32[1,512,512]{2,1,0:T(8,128)} fusion(bf16[8192,512]{1,0:T(8,128)(2,1)} %bitcast_select_fusion, f32[8192,512]{1,0:T(8,128)} %get-tuple-element.120), kind=kOutput, calls=%fused_computation.49 | convolution fusion | flops 4332716032 | bytes 26214400 | tf_op jit(solution)/shard_map/lrf,lrd->lfd/dot_general | solution.py:200
  583.4 11.2 %convolution_bitcast_fusion.1 = f32[1,512,512]{2,1,0:T(8,128)} fusion(bf16[8192,512]{1,0:T(8,128)(2,1)} %bitcast.140, bf16[8192,512]{1,0:T(8,128)(2,1)} %copy-done.47), kind=kOutput, calls=%fused_computation.50 | convolution fusion | flops 4294967296 | bytes 17825792 | tf_op jit(solution)/shard_map/lrd,lrf->ldf/dot_general | solution.py:203
  609.5 63.4 %all-reduce = (f32[512]{0:T(512)}, f32[512]{0:T(512)}, f32[512]{0:T(512)}, f32[512]{0:T(512)}) all-reduce(f32[512]{0:T(512)S(1)} %get-tuple-element.92, f32[512]{0:T(512)S(1)} %get-tuple-element.124, f32[512]{0:T(512)S(1)} %get-tuple-element.88, f32[512]{0:T(512)S(1)} %get-tuple-element.96), channel_id=1, replica_groups=mesh['expert'=4,'dp'=32] {'expert','dp'}, use_global_device_ids=true, to_apply=%region_26.27 | all-reduce | flops 2048 | bytes 16384 | tf_op jit(solution)/shard_map/psum | solution.py:235
  672.9 63.1 %all-reduce.4.cloned.1.call-done = (f32[512,1536]{1,0:T(8,128)}, f32[512,512]{1,0:T(8,128)}, f32[512,32]{0,1:T(8,128)}) async-done(((f32[512,1536]{1,0:T(8,128)}, f32[512,512]{1,0:T(8,128)}, f32[512,32]{0,1:T(8,128)}), (f32[512,1536]{1,0:T(8,128)}, f32[512,512]{1,0:T(8,128)}, f32[512,32]{0,1:T(8,128)})) %all-reduce.4.cloned.1.call-update) | async-done | bytes 4259856 | tf_op jit(solution)/shard_map/psum | solution.py:235
  (222 shorter events, 138.4 us)
Async XLA Ops:
  8.0 36.3 %copy-start = (bf16[512,1536]{1,0:T(8,128)(2,1)S(1)}, bf16[512,1536]{1,0:T(8,128)(2,1)}, u32[]{:S(2)}) copy-start(bf16[512,1536]{1,0:T(8,128)(2,1)} %param.20) | copy-start | bytes 4718596
  8.0 32.8 %copy-start.23 = (s32[512,2]{0,1:T(2,128)S(1)}, s32[512,2]{0,1:T(2,128)}, u32[]{:S(2)}) copy-start(s32[512,2]{0,1:T(2,128)} %param.16) | copy-start | bytes 12292
  8.0 33.3 %copy-start.39 = (s32[1,512]{1,0:T(1,128)S(1)}, s32[1,512]{1,0:T(1,128)}, u32[]{:S(2)}) copy-start(s32[1,512]{1,0:T(1,128)} %param.15) | copy-start | bytes 6148
  8.0 33.5 %copy-start.18 = (bf16[512,512]{1,0:T(8,128)(2,1)S(1)}, bf16[512,512]{1,0:T(8,128)(2,1)}, u32[]{:S(2)}) copy-start(bf16[512,512]{1,0:T(8,128)(2,1)} %param.14) | copy-start | bytes 1572868
  8.1 34.0 %copy-start.19 = (bf16[512,512]{1,0:T(8,128)(2,1)S(1)}, bf16[512,512]{1,0:T(8,128)(2,1)}, u32[]{:S(2)}) copy-start(bf16[512,512]{1,0:T(8,128)(2,1)} %param.27) | copy-start | bytes 1572868
  8.1 36.3 %copy-start.40 = (f32[512]{0:T(512)S(1)}, f32[512]{0:T(512)}, u32[]{:S(2)}) copy-start(f32[512]{0:T(512)} %param.18) | copy-start | bytes 6148
  8.1 36.3 %copy-start.45 = (f32[512]{0:T(512)S(1)}, f32[512]{0:T(512)}, u32[]{:S(2)}) copy-start(f32[512]{0:T(512)} %param.19) | copy-start | bytes 6148
  32.0 66.5 %all-to-all-start = ((s32[32,1,64]{2,1,0:T(1,128)}), s32[32,1,64]{2,1,0:T(1,128)S(1)}, u32[]{:S(2)}, u32[]{:S(2)}) async-start(s32[32,1,64]{2,1,0:T(1,128)} %bitcast.12), calls=%async_computation | async-start | bytes 32768 | tf_op jit(solution)/shard_map/all_to_all | solution.py:149
  41.8 20.6 %copy-start.4 = (bf16[512,512]{0,1:T(8,128)(2,1)}, bf16[512,512]{0,1:T(8,128)(2,1)S(1)}, u32[]{:S(2)}) copy-start(bf16[512,512]{0,1:T(8,128)(2,1)S(1)} %copy.190) | copy-start | bytes 1572868
  98.5 117.6 %copy-start.44 = (bf16[1,512,512]{2,1,0:T(8,128)(2,1)S(1)}, bf16[1,512,512]{2,1,0:T(8,128)(2,1)}, u32[]{:S(2)}) copy-start(bf16[1,512,512]{2,1,0:T(8,128)(2,1)} %param.26) | copy-start | bytes 1572868
  98.5 35.9 %all-to-all-start.3 = ((bf16[32,64,512]{2,1,0:T(8,128)(2,1)}), bf16[32,64,512]{2,1,0:T(8,128)(2,1)}, u32[]{:S(2)}, u32[]{:S(2)}) async-start(bf16[32,64,512]{2,1,0:T(8,128)(2,1)} %get-tuple-element.111), calls=%async_computation.4 | async-start | bytes 4194304 | tf_op jit(solution)/shard_map/all_to_all | solution.py:187
  106.1 62.0 %top_k.9.cloned.1.call-start = ((), (), s32[]{:S(2)}) async-start(), calls=%async_computation.12 | async-start | bytes 98336 | tf_op jit(solution)/shard_map/top_k | solution.py:158
  118.5 97.7 %all-gather.6.cloned.1.call-start = ((), (), s32[]{:S(2)}) async-start(), calls=%async_computation.9 | async-start | bytes 10485760 | tf_op jit(solution)/shard_map/all_gather | solution.py:188
  134.5 167.2 %all-gather.4.cloned.1.call-start = ((), (), s32[]{:S(2)}) async-start(), calls=%async_computation.7 | async-start | bytes 10485760 | tf_op jit(solution)/shard_map/all_gather | solution.py:152
  168.1 247.4 %reduce-scatter.5.cloned.1.call-start = ((), (), s32[]{:S(2)}) async-start(), calls=%async_computation.10 | async-start | bytes 10485760 | tf_op jit(solution)/shard_map/reduce_scatter | solution.py:206
  216.1 85.6 %copy-start.43 = (bf16[1,512,512]{2,1,0:T(8,128)(2,1)S(1)}, bf16[1,512,512]{2,1,0:T(8,128)(2,1)}, u32[]{:S(2)}) copy-start(bf16[1,512,512]{2,1,0:T(8,128)(2,1)} %param.25) | copy-start | bytes 1572868
  333.8 164.4 %reduce-scatter.3.cloned.1.call-start = ((), (), s32[]{:S(2)}) async-start(), calls=%async_computation.8 | async-start | bytes 10485760 | tf_op jit(solution)/shard_map/reduce_scatter | solution.py:169
  347.7 171.0 %copy-start.28 = (s32[1024]{0:T(1024)}, s32[1024]{0:T(1024)S(1)}, u32[]{:S(2)}) copy-start(s32[1024]{0:T(1024)S(1)} %broadcast_clamp_fusion.1) | copy-start | bytes 12292
  419.5 78.7 %all-to-all-start.4 = ((bf16[32,64,512]{2,1,0:T(8,128)(2,1)}), bf16[32,64,512]{2,1,0:T(8,128)(2,1)}, u32[]{:S(2)}, u32[]{:S(2)}) async-start(bf16[32,64,512]{2,1,0:T(8,128)(2,1)} %copy.208), calls=%async_computation.6 | async-start | bytes 4194304 | tf_op jit(solution)/shard_map/all_to_all | solution.py:209
  498.1 36.0 %all-to-all-start.2 = ((bf16[32,64,512]{2,1,0:T(8,128)(2,1)}), bf16[32,64,512]{2,1,0:T(8,128)(2,1)}, u32[]{:S(2)}, u32[]{:S(2)}) async-start(bf16[32,64,512]{2,1,0:T(8,128)(2,1)} %reduce-scatter.3.cloned.1.call-done), calls=%async_computation.3 | async-start | bytes 4194304 | tf_op jit(solution)/shard_map/all_to_all | solution.py:172
  505.8 230.2 %all-reduce.4.cloned.1.call-start = ((), (), s32[]{:S(2)}) async-start(), calls=%async_computation.11 | async-start | bytes 8519680 | tf_op jit(solution)/shard_map/psum | solution.py:235
  534.1 19.4 %copy-start.17 = (f32[512,32]{0,1:T(8,128)S(1)}, f32[512,32]{0,1:T(8,128)}, u32[]{:S(2)}) copy-start(f32[512,32]{0,1:T(8,128)} %copy-done.16) | copy-start | bytes 196612
  534.1 20.1 %copy-start.11 = (bf16[512,512]{0,1:T(8,128)(2,1)S(1)}, bf16[512,512]{0,1:T(8,128)(2,1)}, u32[]{:S(2)}) copy-start(bf16[512,512]{0,1:T(8,128)(2,1)} %copy-done.10) | copy-start | bytes 1572868
  534.2 21.3 %copy-start.3 = (f32[512,512]{0,1:T(8,128)S(1)}, f32[512,512]{0,1:T(8,128)}, u32[]{:S(2)}) copy-start(f32[512,512]{0,1:T(8,128)} %copy-done.2) | copy-start | bytes 3145732
  (36 other events, 169.6 us)
Sparse Core Ops, SparseCore 0:
  118.6 14.6 top_k.11.cloned.1.call-done
  583.5 152.4 all-reduce.3
  (1 shorter events, 0.0 us)
Sparse Core Ops, SparseCore 1:
  134.6 81.5 all-gather.5
  217.6 84.0 all-gather.3
  333.8 81.5 reduce-scatter.4
  417.9 80.2 reduce-scatter.2
where the time goes:
time: 755 us; the launch traced here: 751 us
  waiting for transfers between devices  333 us (44%)
  matrix products  108 us (14%)
  blocking collectives  108 us (14%)
  local copies, waits for them, and re-layouts  102 us (14%)
  other arithmetic  49.2 us (7%)
  starting transfers between devices  32.1 us (4%)
  between operations  17.5 us (2%)
    all_gather x1, waiting for transfers between devices, per_device(): lax.all_gather(moved_rows, 'expert', axis=0, tiled=True)  75.2 us
    reduce_scatter x1, waiting for transfers between devices, per_device(): lax.psum_scatter(grad_outgoing.astype(jnp.bfloat16), 'expert', scatter_di...  67.7 us
    reduce_scatter x1, waiting for transfers between devices, per_device(): lax.psum_scatter(outgoing.astype(jnp.bfloat16), 'expert', scatter_dimensi...  63.5 us
    psum x1, blocking collectives, per_device(): lax.psum((d_gain1, d_shift1, d_w_qkv, d_w_out, d_gain2, d_shift2, d_route...  63.4 us
    psum x1, waiting for transfers between devices, per_device(): lax.psum((d_gain1, d_shift1, d_w_qkv, d_w_out, d_gain2, d_shift2, d_route...  63.1 us
    all_gather x1, waiting for transfers between devices, per_device(): recv_grad = lax.all_gather(moved_grad, 'expert', axis=0, tiled=True)  45.7 us
    all_to_all x1, blocking collectives, per_device(): lax.all_to_all(send_rows, 'dp', split_axis=0, concat_axis=0, tiled=True)  33.5 us
    dot_general x1, matrix products, per_device(): jnp.einsum('lrd,ldf->lrf', expert_rows, first_full, preferred_element_typ...  20.8 us
  transfers between devices with their start and end apart: 9, of which 7 were waited for; matrix products, arithmetic and copies ran while one was open for 19% of the time, Pallas kernels for 0%

commit v1 on v0

v1 whole, which is shorter than its diff:
```python
import functools

import jax
import jax.numpy as jnp
from jax import lax
from jax.experimental import pallas as pl
from jax.experimental.pallas import tpu as pltpu
from jax.sharding import PartitionSpec as P

D = 512
HEADS = 8
HDIM = 64
EXPERTS = 32
MOST = 64
ROWS = 512
SLOTS = EXPERTS * MOST
N_Z = 4
N_DP = 32
CAP = (21 * N_Z * N_DP * ROWS + 319) // 320
TOKENS = N_Z * N_DP * ROWS
EXTRA = 8
EPS = 1e-06
SCALE = HDIM ** (-0.5)
STARTS = (0, 64, 192, 256)
GELU_C = 0.7978845608028654
GELU_A = 0.044715

bf16 = jnp.bfloat16
f32 = jnp.float32
VMEM_LIMIT = 56 * 1024 * 1024


def dot(a, b):
    return lax.dot_general(a, b, (((1,), (0,)), ((), ())), preferred_element_type=f32)


def dot_nt(a, b):
    return lax.dot_general(a, b, (((1,), (1,)), ((), ())), preferred_element_type=f32)


def dot_tn(a, b):
    return lax.dot_general(a, b, (((0,), (0,)), ((), ())), preferred_element_type=f32)


def iota(shape, dim):
    return lax.broadcasted_iota(jnp.int32, shape, dim)


def normalize(values):
    center = values - jnp.mean(values, axis=-1, keepdims=True)
    factor = lax.rsqrt(jnp.mean(center * center, axis=-1, keepdims=True) + EPS)
    return center * factor, factor


def norm_backward(upstream, normal, factor, gain):
    scaled = upstream * gain
    inner = (
        scaled
        - jnp.mean(scaled, axis=-1, keepdims=True)
        - normal * jnp.mean(scaled * normal, axis=-1, keepdims=True)
    )
    return (
        inner * factor,
        jnp.sum(upstream * normal, axis=0, keepdims=True),
        jnp.sum(upstream, axis=0, keepdims=True),
    )


def pick_rows(csel_ref, rows, store):
    place = iota((MOST, ROWS), 0).astype(f32)
    for group in range(EXPERTS // 4):
        parts = []
        for j in range(4):
            line = csel_ref[group * 4 + j : group * 4 + j + 1, :]
            parts.append((place == line).astype(f32).astype(bf16))
        hot = jnp.concatenate(parts, axis=0)
        store(group, dot(hot, rows).astype(bf16))


def pack_kernel(routes_ref, prio_ref, seg_ref, cot_ref, send_ref, csel_ref, cols_ref, wide_ref):
    routes = routes_ref[...]
    experts = iota((EXPERTS, ROWS), 0)
    first = routes[0:1] == experts
    second = routes[1:2] == experts
    either = jnp.logical_or(first, second)
    before = (iota((ROWS, ROWS), 0) < iota((ROWS, ROWS), 1)).astype(f32).astype(bf16)
    count = dot(either.astype(f32).astype(bf16), before)
    slot = count + (experts * MOST).astype(f32)
    wide_ref[...] = jnp.zeros_like(wide_ref)
    wide_ref[0:1, :] = jnp.sum(jnp.where(first, slot, 0.0), axis=0, keepdims=True)
    wide_ref[1:2, :] = jnp.sum(jnp.where(second, slot, 0.0), axis=0, keepdims=True)
    wide_ref[2:3, :] = prio_ref[...].astype(f32)
    wide_ref[3:4, :] = seg_ref[...].astype(f32)
    csel_ref[...] = jnp.where(either, count, -1.0)
    cols = wide_ref[...].T
    cols_ref[...] = cols
    cols_int = cols[:, 0:3].astype(jnp.int32)
    pos0, pos1, key = cols_int[:, 0:1], cols_int[:, 1:2], cols_int[:, 2:3] + 1
    zeros = jnp.zeros((EXTRA, D), bf16)
    digit = iota((EXTRA, 256), 0)

    def store(group, rows):
        send_ref[group * 4 : group * 4 + 4, 0:MOST, :] = rows.reshape(4, MOST, D)
        spot = iota((ROWS, 256), 1) + group * 256
        keys = jnp.sum(
            jnp.where(spot == pos0, key, 0) + jnp.where(spot == pos1, key + TOKENS, 0),
            axis=0,
            keepdims=True,
        )
        low = jnp.bitwise_and(keys, 255)
        mid = jnp.bitwise_and(jnp.right_shift(keys, 8), 255)
        high = jnp.right_shift(keys, 16)
        digits = jnp.where(
            digit == 0, low, jnp.where(digit == 1, mid, jnp.where(digit == 2, high, 0))
        ).astype(f32)
        for j in range(4):
            send_ref[group * 4 + j, MOST : MOST + EXTRA, :] = zeros
            send_ref[group * 4 + j, MOST : MOST + EXTRA, 0:MOST] = digits[
                :, j * MOST : (j + 1) * MOST
            ].astype(bf16)

    pick_rows(csel_ref, cot_ref[...], store)


def stacked(pair):
    lanes = iota(pair.shape, 1)
    zero = jnp.zeros_like(pair)
    return jnp.concatenate(
        [jnp.where(lanes < HDIM, pair, zero), jnp.where(lanes >= HDIM, pair, zero)], axis=0
    )


def band_bias(cols_ref, seg_ref, block):
    start = STARTS[block]
    same = (
        cols_ref[block * 128 : block * 128 + 128, 3:4]
        == seg_ref[:, start : start + 256].astype(f32)
    )
    bias = jnp.where(same, 0.0, -1e30)
    return jnp.concatenate([bias, bias], axis=0)


def attend_kernel(
    tokens_ref,
    seg_ref,
    cols_ref,
    csel_ref,
    gain1_ref,
    bias1_ref,
    w_qkv_ref,
    w_out_ref,
    gain2_ref,
    bias2_ref,
    packed_ref,
    attended_ref,
    lse_ref,
    residual_ref,
    send_ref,
):
    inputs = tokens_ref[...].astype(f32)
    normal, _ = normalize(inputs)
    first = (normal * gain1_ref[...] + bias1_ref[...]).astype(bf16)
    for part in range(3):
        packed_ref[:, part * D : (part + 1) * D] = dot(
            first, w_qkv_ref[:, part * D : (part + 1) * D]
        ).astype(bf16)
    lanes = iota((128, 128), 1)
    for block in range(4):
        here = slice(block * 128, block * 128 + 128)
        window = slice(STARTS[block], STARTS[block] + 256)
        bias = band_bias(cols_ref, seg_ref, block)
        lse = jnp.zeros((128, 128), f32)
        for pair in range(4):
            at = pair * 128
            query = stacked(packed_ref[here, at : at + 128])
            scores = dot_nt(query, packed_ref[window, D + at : D + at + 128]) * SCALE + bias
            highest = jnp.max(scores, axis=-1, keepdims=True)
            raised = jnp.exp(scores - highest)
            total = jnp.sum(raised, axis=-1, keepdims=True)
            weights = (raised * (1.0 / total)).astype(bf16)
            mixed = dot(weights, packed_ref[window, 2 * D + at : 2 * D + at + 128])
            attended_ref[here, at : at + 128] = jnp.where(
                lanes < HDIM, mixed[0:128], mixed[128:256]
            ).astype(bf16)
            logsum = highest + jnp.log(total)
            lse = jnp.where(lanes == 2 * pair, logsum[0:128], lse)
            lse = jnp.where(lanes == 2 * pair + 1, logsum[128:256], lse)
        lse_ref[here, :] = lse
    residual = inputs + dot(attended_ref[...], w_out_ref[...])
    residual_ref[...] = residual
    normal2, _ = normalize(residual)
    second = (normal2 * gain2_ref[...] + bias2_ref[...]).astype(bf16)

    def store(group, rows):
        send_ref[group * 4 : group * 4 + 4] = rows.reshape(4, MOST, D)

    pick_rows(csel_ref, second, store)


def keep_kernel(all_ref, own_ref, kept_ref):
    empty = 2 * TOKENS + 1
    keys = all_ref[...]
    keys = jnp.where(keys == 0, empty, keys)

    def step(_, bounds):
        low, high = bounds
        middle = jnp.right_shift(low + high, 1)
        enough = jnp.sum((keys <= middle).astype(jnp.int32), keepdims=True) >= CAP
        return jnp.where(enough, low, middle + 1), jnp.where(enough, middle, high)

    low = jnp.zeros((1, 1), jnp.int32)
    high = jnp.full((1, 1), 2 * TOKENS, jnp.int32)
    low, high = lax.fori_loop(0, 18, step, (low, high))
    own = own_ref[...]
    kept_ref[...] = jnp.logical_and(own > 0, own <= high).astype(f32)


def back_kernel(grad_ref, w2_ref, out_ref):
    rows = grad_ref[...].reshape(256, D)
    for part in range(4):
        out_ref[:, part * 512 : part * 512 + 512] = dot_nt(rows, w2_ref[part]).astype(bf16)


def slot_kernel(
    expert_ref,
    x_ref,
    gw_ref,
    w1_ref,
    kept_ref,
    w_router_ref,
    dslot_ref,
    act_ref,
    dpre_ref,
    scale_ref,
    d_router_ref,
):
    rows = x_ref[...].reshape(256, D)
    logits = dot(rows, w_router_ref[...])
    raised = jnp.exp(logits - jnp.max(logits, axis=-1, keepdims=True))
    prob = raised / jnp.sum(raised, axis=-1, keepdims=True)
    mine = iota((256, EXPERTS), 1) == expert_ref[0]
    gate = jnp.sum(jnp.where(mine, prob, 0.0), axis=-1, keepdims=True)
    kept = kept_ref[...]
    scale = kept * gate
    scale_ref[...] = scale
    dslot = jnp.zeros((256, D), f32)
    dgate = jnp.zeros((256, 1), f32)
    for part in range(4):
        span = slice(part * 512, part * 512 + 512)
        weight = w1_ref[part]
        pre = dot(rows, weight)
        square = pre * pre
        bend = jnp.tanh(GELU_C * pre * (1.0 + GELU_A * square))
        half = 0.5 * (1.0 + bend)
        act = pre * half
        slope = half + 0.5 * pre * (1.0 - bend * bend) * (
            GELU_C + (3.0 * GELU_A * GELU_C) * square
        )
        upstream = gw_ref[:, span].astype(f32)
        dgate = dgate + jnp.sum(upstream * act, axis=-1, keepdims=True)
        dpre = (upstream * scale * slope).astype(bf16)
        act_ref[:, span] = act.astype(bf16)
        dpre_ref[:, span] = dpre
        dslot = dslot + dot_nt(dpre, weight)
    dlogit = (kept * dgate * gate * (mine.astype(f32) - prob)).astype(bf16)
    dslot = dslot + dot_nt(dlogit, w_router_ref[...])
    dslot_ref[...] = dslot.astype(bf16).reshape(4, MOST, D)

    @pl.when(pl.program_id(0) == 0)
    def _():
        d_router_ref[...] = jnp.zeros_like(d_router_ref)

    d_router_ref[...] += dot_tn(dlogit, rows)


def out_kernel(act_ref, w2_ref, scale_ref, y_ref):
    total = jnp.zeros((256, D), f32)
    for part in range(4):
        total = total + dot(act_ref[:, part * 512 : part * 512 + 512], w2_ref[part])
    y_ref[...] = (total * scale_ref[...]).astype(bf16).reshape(4, MOST, D)


def weight_kernel(x_ref, grad_ref, scale_ref, act_ref, dpre_ref, out_ref):
    rows = x_ref[...].reshape(SLOTS, D)
    out_ref[0, 0] = dot_tn(rows, dpre_ref[...]).astype(bf16)
    upstream = (grad_ref[...].reshape(SLOTS, D).astype(f32) * scale_ref[...]).astype(bf16)
    out_ref[0, 1] = dot_tn(act_ref[...], upstream).astype(bf16)


def gather_slots(cols_ref, rows_ref):
    pos0 = cols_ref[:, 0:1].astype(jnp.int32)
    pos1 = cols_ref[:, 1:2].astype(jnp.int32)
    total = jnp.zeros((ROWS, D), f32)
    for part in range(4):
        spot = iota((ROWS, 512), 1) + part * 512
        hot = jnp.logical_or(spot == pos0, spot == pos1).astype(f32).astype(bf16)
        total = total + dot(hot, rows_ref[part * 8 : part * 8 + 8].reshape(512, D))
    return total


def backward_kernel(
    dslot_ref,
    cols_ref,
    seg_ref,
    tokens_ref,
    cot_ref,
    residual_ref,
    packed_ref,
    attended_ref,
    lse_ref,
    gain1_ref,
    bias1_ref,
    w_qkv_ref,
    w_out_ref,
    gain2_ref,
    d_router_ref,
    grads_ref,
    d_tokens_ref,
    datt_ref,
    dpacked_ref,
    dkey_ref,
    dvalue_ref,
):
    d_second = gather_slots(cols_ref, dslot_ref)
    normal2, factor2 = normalize(residual_ref[...])
    d_norm2, d_gain2, d_shift2 = norm_backward(d_second, normal2, factor2, gain2_ref[...])
    d_residual = cot_ref[...].astype(f32) + d_norm2
    d_tokens_ref[...] = d_residual
    d_branch = d_residual.astype(bf16)
    grads_ref[3 * D : 4 * D, :] = dot_tn(attended_ref[...], d_branch).astype(bf16)
    datt_ref[...] = dot_nt(d_branch, w_out_ref[...]).astype(bf16)
    lanes = iota((128, 128), 1)
    for pair in range(4):
        at = pair * 128
        dkey_ref[...] = jnp.zeros_like(dkey_ref)
        dvalue_ref[...] = jnp.zeros_like(dvalue_ref)
        for block in range(4):
            here = slice(block * 128, block * 128 + 128)
            window = slice(STARTS[block], STARTS[block] + 256)
            bias = band_bias(cols_ref, seg_ref, block)
            query = stacked(packed_ref[here, at : at + 128])
            upstream = stacked(datt_ref[here, at : at + 128])
            keys = packed_ref[window, D + at : D + at + 128]
            values = packed_ref[window, 2 * D + at : 2 * D + at + 128]
            logsum = jnp.concatenate(
                [
                    lse_ref[here, 2 * pair : 2 * pair + 1],
                    lse_ref[here, 2 * pair + 1 : 2 * pair + 2],
                ],
                axis=0,
            )
            weights = jnp.exp(dot_nt(query, keys) * SCALE + bias - logsum)
            d_weights = dot_nt(upstream, values)
            inner = jnp.sum(weights * d_weights, axis=-1, keepdims=True)
            d_scores = (weights * (d_weights - inner)).astype(bf16)
            d_query = dot(d_scores, keys) * SCALE
            dpacked_ref[here, at : at + 128] = jnp.where(
                lanes < HDIM, d_query[0:128], d_query[128:256]
            ).astype(bf16)
            dkey_ref[window, :] += dot_tn(d_scores, query)
            dvalue_ref[window, :] += dot_tn(weights.astype(bf16), upstream)
        dpacked_ref[:, D + at : D + at + 128] = (dkey_ref[...] * SCALE).astype(bf16)
        dpacked_ref[:, 2 * D + at : 2 * D + at + 128] = dvalue_ref[...].astype(bf16)
    normal1, factor1 = normalize(tokens_ref[...].astype(f32))
    first = (normal1 * gain1_ref[...] + bias1_ref[...]).astype(bf16)
    for part in range(3):
        grads_ref[part * D : (part + 1) * D, :] = dot_tn(
            first, dpacked_ref[:, part * D : (part + 1) * D]
        ).astype(bf16)
    d_first = dot_nt(dpacked_ref[...], w_qkv_ref[...])
    d_norm1, d_gain1, d_shift1 = norm_backward(d_first, normal1, factor1, gain1_ref[...])
    d_tokens_ref[...] += d_norm1
    grads_ref[4 * D :, :] = jnp.zeros((grads_ref.shape[0] - 4 * D, D), bf16)
    row = iota((16, D), 0)
    small = jnp.where(
        row == 0,
        d_gain1,
        jnp.where(
            row == 1, d_shift1, jnp.where(row == 2, d_gain2, jnp.where(row == 3, d_shift2, 0.0))
        ),
    )
    grads_ref[4 * D : 4 * D + 16, :] = small.astype(bf16)
    grads_ref[4 * D + 16 : 4 * D + 16 + EXPERTS, :] = d_router_ref[...].astype(bf16)


def output_kernel(y_ref, cols_ref, residual_ref, out_ref):
    out_ref[...] = (residual_ref[...] + gather_slots(cols_ref, y_ref)).astype(bf16)


def params():
    return pltpu.CompilerParams(vmem_limit_bytes=VMEM_LIMIT)


def call(kernel, out_shape, *args, flops=0, scratch=()):
    shapes = jax.tree.leaves(out_shape)
    moved = sum(a.size * a.dtype.itemsize for a in args) + sum(
        s.size * s.dtype.itemsize for s in shapes
    )
    return pl.pallas_call(
        kernel,
        out_shape=out_shape,
        scratch_shapes=list(scratch),
        compiler_params=params(),
        cost_estimate=pl.CostEstimate(flops=flops, bytes_accessed=moved, transcendentals=0),
    )(*args)


def shape(dims, dtype):
    return jax.ShapeDtypeStruct(dims, dtype)


def shift(axis, distance):
    pairs = []
    for x in range(4):
        for y in range(4):
            for core in range(2):
                to = {
                    "x": ((x + distance) % 4, y, core),
                    "y": (x, (y + distance) % 4, core),
                    "core": (x, y, (core + distance) % 2),
                }[axis]
                pairs.append(((x * 4 + y) * 2 + core, (to[0] * 4 + to[1]) * 2 + to[2]))
    return pairs


def sum_everywhere(grads):
    index = lax.axis_index("dp")
    core, y, x = index % 2, (index // 2) % 4, index // 8
    half = grads.shape[0] // 2

    def piece(values, which, size):
        return lax.dynamic_slice_in_dim(values, which * size, size, axis=0)

    got = lax.ppermute(piece(grads, 1 - core, half), "dp", shift("core", 1))
    total = piece(grads, core, half).astype(f32) + got.astype(f32)
    for axis, where in (("x", x), ("y", y)):
        size = total.shape[0] // 4
        low = total.astype(bf16)
        got = [
            lax.ppermute(piece(low, (where + d) % 4, size), "dp", shift(axis, d))
            for d in (1, 2, 3)
        ]
        total = piece(total, where, size)
        for part in got:
            total = total + part.astype(f32)
    low = total.astype(bf16)
    got = [
        lax.ppermute(low, "expert", [(i, (i + d) % 4) for i in range(4)]).astype(f32)
        for d in (1, 2, 3)
    ]
    low = ((low.astype(f32) + got[1]) + (got[0] + got[2])).astype(bf16)
    for axis, where in (("y", y), ("x", x)):
        size = low.shape[0]
        whole = jnp.zeros((4 * size, D), bf16)
        whole = lax.dynamic_update_slice_in_dim(whole, low, where * size, axis=0)
        for d in (1, 2, 3):
            part = lax.ppermute(low, "dp", shift(axis, d))
            whole = lax.dynamic_update_slice_in_dim(
                whole, part, ((where - d) % 4) * size, axis=0
            )
        low = whole
    other = lax.ppermute(low, "dp", shift("core", 1))
    return jnp.where(
        core == 0,
        jnp.concatenate([low, other], axis=0),
        jnp.concatenate([other, low], axis=0),
    )


def per_device(
    tokens,
    segments,
    routes,
    priority,
    ln1_gain,
    ln1_bias,
    w_qkv,
    w_out,
    ln2_gain,
    ln2_bias,
    w_router,
    expert_in,
    expert_out,
    cotangent,
):
    gain1, bias1 = ln1_gain.reshape(1, D), ln1_bias.reshape(1, D)
    gain2, bias2 = ln2_gain.reshape(1, D), ln2_bias.reshape(1, D)
    w2 = lax.all_gather(expert_out[0], "expert", axis=0)
    w1 = lax.all_gather(expert_in[0], "expert", axis=0)

    send_grad, csel, cols = call(
        pack_kernel,
        (
            shape((EXPERTS, MOST + EXTRA, D), bf16),
            shape((EXPERTS, ROWS), f32),
            shape((ROWS, 128), f32),
        ),
        routes.T,
        priority.reshape(1, ROWS),
        segments,
        cotangent,
        flops=2 * SLOTS * D * D,
        scratch=[pltpu.VMEM((128, ROWS), f32)],
    )
    grad = lax.all_to_all(send_grad, "dp", split_axis=0, concat_axis=0, tiled=True)

    packed, attended, lse, residual, send_rows = call(
        attend_kernel,
        (
            shape((ROWS, 3 * D), bf16),
            shape((ROWS, D), bf16),
            shape((ROWS, 128), f32),
            shape((ROWS, D), f32),
            shape((EXPERTS, MOST, D), bf16),
        ),
        tokens,
        segments,
        cols,
        csel,
        gain1,
        bias1,
        w_qkv,
        w_out,
        gain2,
        bias2,
        flops=2 * SLOTS * D * D + 10 * ROWS * D * D,
    )
    rows = lax.all_to_all(send_rows, "dp", split_axis=0, concat_axis=0, tiled=True)

    digits = grad[:, MOST : MOST + 3, 0:MOST].astype(jnp.int32)
    keys = digits[:, 0] + 256 * digits[:, 1] + 65536 * digits[:, 2]
    all_keys = lax.all_gather(keys, "expert", axis=0, tiled=True)
    kept = call(
        keep_kernel,
        shape((N_DP // 2, 128), f32),
        all_keys.reshape(N_Z * N_DP // 2, 128),
        keys.reshape(N_DP // 2, 128),
    ).reshape(SLOTS, 1)

    steps = SLOTS // 256
    any_spec = pl.BlockSpec((4, D, 512), lambda i: (0, 0, 0))
    row_spec = pl.BlockSpec((4, MOST, D), lambda i: (i, 0, 0))
    wide_spec = pl.BlockSpec((256, 2048), lambda i: (i, 0))
    col_spec = pl.BlockSpec((256, 1), lambda i: (i, 0))
    big = 2 * SLOTS * D * 2048
    back = pl.pallas_call(
        back_kernel,
        grid=(steps,),
        in_specs=[row_spec, any_spec],
        out_specs=wide_spec,
        out_shape=shape((SLOTS, 2048), bf16),
        compiler_params=params(),
        cost_estimate=pl.CostEstimate(flops=big, bytes_accessed=12 << 20, transcendentals=0),
    )(grad, w2)
    expert = lax.axis_index("dp").astype(jnp.int32).reshape(1)
    dslot, act, dpre, scale, d_router = pl.pallas_call(
        slot_kernel,
        grid=(steps,),
        in_specs=[
            pl.BlockSpec(memory_space=pltpu.SMEM),
            row_spec,
            wide_spec,
            any_spec,
            col_spec,
            pl.BlockSpec((D, EXPERTS), lambda i: (0, 0)),
        ],
        out_specs=[
            row_spec,
            wide_spec,
            wide_spec,
            col_spec,
            pl.BlockSpec((EXPERTS, D), lambda i: (0, 0)),
        ],
        out_shape=(
            shape((EXPERTS, MOST, D), bf16),
            shape((SLOTS, 2048), bf16),
            shape((SLOTS, 2048), bf16),
            shape((SLOTS, 1), f32),
            shape((EXPERTS, D), f32),
        ),
        compiler_params=params(),
        cost_estimate=pl.CostEstimate(
            flops=2 * big, bytes_accessed=32 << 20, transcendentals=SLOTS * 2048
        ),
    )(expert, rows, back, w1, kept, w_router)
    dslot_home = lax.all_to_all(dslot, "dp", split_axis=0, concat_axis=0, tiled=True)

    y = pl.pallas_call(
        out_kernel,
        grid=(steps,),
        in_specs=[wide_spec, any_spec, col_spec],
        out_specs=row_spec,
        out_shape=shape((EXPERTS, MOST, D), bf16),
        compiler_params=params(),
        cost_estimate=pl.CostEstimate(flops=big, bytes_accessed=12 << 20, transcendentals=0),
    )(act, w2, scale)
    y_home = lax.all_to_all(y, "dp", split_axis=0, concat_axis=0, tiled=True)

    d_weights = pl.pallas_call(
        weight_kernel,
        grid=(N_Z,),
        in_specs=[
            pl.BlockSpec((EXPERTS, MOST, D), lambda i: (0, 0, 0)),
            pl.BlockSpec((EXPERTS, MOST, D), lambda i: (0, 0, 0)),
            pl.BlockSpec((SLOTS, 1), lambda i: (0, 0)),
            pl.BlockSpec((SLOTS, 512), lambda i: (0, i)),
            pl.BlockSpec((SLOTS, 512), lambda i: (0, i)),
        ],
        out_specs=pl.BlockSpec((1, 2, D, 512), lambda i: (i, 0, 0, 0)),
        out_shape=shape((N_Z, 2, D, 512), bf16),
        compiler_params=params(),
        cost_estimate=pl.CostEstimate(flops=2 * big, bytes_accessed=24 << 20, transcendentals=0),
    )(rows, grad, scale, act, dpre)
    d_own = lax.psum_scatter(d_weights, "expert", scatter_dimension=0, tiled=True)

    grads, d_tokens = call(
        backward_kernel,
        (shape((2304, D), bf16), shape((ROWS, D), f32)),
        dslot_home,
        cols,
        segments,
        tokens,
        cotangent,
        residual,
        packed,
        attended,
        lse,
        gain1,
        bias1,
        w_qkv,
        w_out,
        gain2,
        d_router,
        flops=2 * SLOTS * D * D + 20 * ROWS * D * D,
        scratch=[
            pltpu.VMEM((ROWS, D), bf16),
            pltpu.VMEM((ROWS, 3 * D), bf16),
            pltpu.VMEM((ROWS, 128), f32),
            pltpu.VMEM((ROWS, 128), f32),
        ],
    )
    output = call(
        output_kernel, shape((ROWS, D), bf16), y_home, cols, residual, flops=2 * SLOTS * D * D
    )
    summed = sum_everywhere(grads).astype(f32)
    d_w_qkv = jnp.concatenate([summed[0:D], summed[D : 2 * D], summed[2 * D : 3 * D]], axis=1)
    small = summed[4 * D :]
    d_own = d_own.astype(f32)
    return (
        output,
        d_tokens,
        small[0],
        small[1],
        d_w_qkv,
        summed[3 * D : 4 * D],
        small[2],
        small[3],
        small[16 : 16 + EXPERTS].T,
        d_own[:, 0],
        d_own[:, 1],
    )


def solution(mesh):
    both = P(("expert", "dp"), None)
    in_specs = (
        both,
        both,
        both,
        P(("expert", "dp")),
        P(),
        P(),
        P(),
        P(),
        P(),
        P(),
        P(),
        P("dp", None, "expert"),
        P("dp", "expert", None),
        both,
    )
    out_specs = (
        both,
        both,
        P(),
        P(),
        P(),
        P(),
        P(),
        P(),
        P(),
        P("dp", None, "expert"),
        P("dp", "expert", None),
    )
    return jax.shard_map(
        per_device, mesh=mesh, in_specs=in_specs, out_specs=out_specs, check_vma=False
    )
```

time: 755 us -> 307 us (0.41)
  waiting for transfers between devices: 333 us -> 96.8 us
  matrix products: 108 us -> 0 us
  Pallas kernels: 0 us -> 101 us
  blocking collectives: 108 us -> 11.7 us
  local copies, waits for them, and re-layouts: 102 us -> 20.2 us
  other arithmetic: 49.2 us -> 10.9 us
  starting transfers between devices: 32.1 us -> 51.3 us
    reduce_scatter x2 -> x1, waiting for transfers between devices: 131 us -> 0.01 us  [per_device(): lax.psum_scatter(d_weights, 'expert', scatter_dimension=0, tiled=True)]
    all_gather x2, waiting for transfers between devices: 121 us -> 0.01 us  [the longest x1 0.01 us: per_device(): w2 = lax.all_gather(expert_out[0], 'expert', axis=0)]
    dot_general x21 -> x0, matrix products: 108 us -> none  [the longest x1 20.8 us: per_device(): jnp.einsum('lrd,ldf->lrf', expert_rows, first_full, preferred_element_typ...]
    pallas_call x0 -> x9, Pallas kernels: none -> 101 us  [the longest x5 37.7 us: call(): pl.pallas_call(kernel, out_shape=out_shape, scratch_shapes=list(scratch),...]
    psum x1 -> x0, blocking collectives: 63.4 us -> none  [per_device(): lax.psum((d_gain1, d_shift1, d_w_qkv, d_w_out, d_gain2, d_shift2, d_route...]
    psum x1 -> x0, waiting for transfers between devices: 63.1 us -> none  [per_device(): lax.psum((d_gain1, d_shift1, d_w_qkv, d_w_out, d_gain2, d_shift2, d_route...]
    ppermute x0 -> x17, waiting for transfers between devices: none -> 60 us  [the longest x6 32.2 us: sum_everywhere(): part = lax.ppermute(low, 'dp', shift(axis, d))]
    gather x11 -> x0, local copies, waits for them, and re-layouts: 52.1 us -> none  [the longest x2 11.2 us: per_device(): priority[token_of]]
  transfers between devices with their start and end apart: 9 -> 24, of which waited for: 7 -> 16; matrix products, arithmetic and copies ran while one was open for 19% -> 8% of each run, Pallas kernels for 0% -> 24%
where the time goes in v1:
time: 307 us; the launch traced here: 306 us
  Pallas kernels  101 us (33%)
  waiting for transfers between devices  96.8 us (32%)
  starting transfers between devices  51.3 us (17%)
  local copies, waits for them, and re-layouts  20.2 us (7%)
  between operations  14 us (5%)
  blocking collectives  11.7 us (4%)
  other arithmetic  10.9 us (4%)
    pallas_call x5, Pallas kernels, call(): pl.pallas_call(kernel, out_shape=out_shape, scratch_shapes=list(scratch),...  37.7 us
    ppermute x6, waiting for transfers between devices, sum_everywhere(): part = lax.ppermute(low, 'dp', shift(axis, d))  32.2 us
    pallas_call x1, Pallas kernels, per_device(): pl.pallas_call(slot_kernel, grid=(steps,), in_specs=[pl.BlockSpec(memory_...  27.6 us
    all_to_all x1, waiting for transfers between devices, per_device(): lax.all_to_all(send_grad, 'dp', split_axis=0, concat_axis=0, tiled=True)  21.8 us
    ppermute x6, waiting for transfers between devices, sum_everywhere(): lax.ppermute(piece(low, (where + d) % 4, size), 'dp', shift(axis, d))  21.3 us
    pallas_call x1, Pallas kernels, per_device(): pl.pallas_call(weight_kernel, grid=(N_Z,), in_specs=[pl.BlockSpec((EXPERT...  14.7 us
    all_to_all x1, waiting for transfers between devices, per_device(): lax.all_to_all(dslot, 'dp', split_axis=0, concat_axis=0, tiled=True)  13.6 us
    all_gather x1, blocking collectives, per_device(): all_keys = lax.all_gather(keys, 'expert', axis=0, tiled=True)  11.7 us
  transfers between devices with their start and end apart: 24, of which 16 were waited for; matrix products, arithmetic and copies ran while one was open for 8% of the time, Pallas kernels for 24%

profile of v1, /device:TPU:1, one launch (start us, length us, event | category | flops | bytes accessed | tf_op | source)
XLA Modules:
  0.0 305.6 jit_solution(2653253270911828262)
XLA Ops:
  7.9 4.8 %shard_map.221 = (bf16[32,72,512]{2,1,0:T(8,128)(2,1)}, f32[32,512]{1,0:T(8,128)}, f32[512,128]{1,0:T(8,128)}) custom-call(s32[2,512]{1,0:T(2,128)} %bitcast.23, s32[1,512]{1,0:T(1,128)} %bitcast.24, s32[1,512]{1,0:T(1,128)} %seg_ref.5, bf16[512,512]{1,0:T(8,128)(2,1)} %cot_ref.3), custom_call_target="tpu_custom_call" | custom-call | flops 1073741824 | bytes 3219456 | tf_op jit(solution)/shard_map/pallas_call | solution.py:399
  12.7 8.6 %all-to-all-start.1 = ((bf16[32,72,512]{2,1,0:T(8,128)(2,1)}), bf16[32,72,512]{2,1,0:T(8,128)(2,1)S(1)}, u32[]{:S(2)}, u32[]{:S(2)}) async-start(bf16[32,72,512]{2,1,0:T(8,128)(2,1)} %get-tuple-element.29), calls=%async_computation.1 | async-start | bytes 4718592 | tf_op jit(solution)/shard_map/all_to_all | solution.py:505
  22.1 8.5 %shard_map.222 = (bf16[512,1536]{1,0:T(8,128)(2,1)}, bf16[512,512]{1,0:T(8,128)(2,1)}, f32[512,128]{1,0:T(8,128)}, f32[512,512]{1,0:T(8,128)}, bf16[32,64,512]{2,1,0:T(8,128)(2,1)}) custom-call(bf16[512,512]{1,0:T(8,128)(2,1)} %tokens_ref.3, s32[1,512]{1,0:T(1,128)} %seg_ref.5, f32[512,128]{1,0:T(8,128)} %get-tuple-element.26.cols_ref, ...), custom_call_target="tpu_custom_call" | custom-call | flops 2415919104 | bytes 8464384 | tf_op jit(solution)/shard_map/pallas_call | solution.py:399
  30.6 21.8 %all-to-all-done.1.grad_ref = bf16[32,72,512]{2,1,0:T(8,128)(2,1)S(1)} async-done(((bf16[32,72,512]{2,1,0:T(8,128)(2,1)}), bf16[32,72,512]{2,1,0:T(8,128)(2,1)S(1)}, u32[]{:S(2)}, u32[]{:S(2)}) %all-to-all-start.1) | async-done | bytes 2359328 | tf_op jit(solution)/shard_map/all_to_all | solution.py:505
  52.5 5.3 %all-to-all-start = ((bf16[32,64,512]{2,1,0:T(8,128)(2,1)}), bf16[32,64,512]{2,1,0:T(8,128)(2,1)}, u32[]{:S(2)}, u32[]{:S(2)}) async-start(bf16[32,64,512]{2,1,0:T(8,128)(2,1)} %get-tuple-element.28), calls=%async_computation | async-start | bytes 4194304 | tf_op jit(solution)/shard_map/all_to_all | solution.py:528
  59.8 11.7 %all-gather = s32[128,1,64]{2,1,0:T(1,128)S(1)} all-gather(s32[32,1,64]{2,1,0:T(1,128)S(1)} %get-tuple-element.48), channel_id=2, replica_groups=mesh['expert'=4,'dp'=32] {'expert'}, dimensions={0}, use_global_device_ids=true | all-gather | bytes 40960 | tf_op jit(solution)/shard_map/all_gather | solution.py:532
  73.7 3.7 %shard_map.224 = f32[16,128]{1,0:T(8,128)} custom-call(s32[64,128]{1,0:T(8,128)} %reshape.68.all_ref, s32[16,128]{1,0:T(8,128)} %add.170.own_ref), custom_call_target="tpu_custom_call" | custom-call | bytes 49152 | tf_op jit(solution)/shard_map/pallas_call | solution.py:399
  79.4 10.3 %shard_map.223.gw_ref = bf16[2048,2048]{1,0:T(8,128)(2,1)} custom-call(bf16[32,72,512]{2,1,0:T(8,128)(2,1)} %copy-done, bf16[4,512,512]{2,1,0:T(8,128)(2,1)} %all-gather.4.cloned.1.call-done.w2_ref), custom_call_target="tpu_custom_call" | custom-call | flops 4294967296 | bytes 12582912 | tf_op jit(solution)/shard_map/pallas_call | solution.py:546
  89.7 27.6 %shard_map.225 = (bf16[32,64,512]{2,1,0:T(8,128)(2,1)}, bf16[2048,2048]{1,0:T(8,128)(2,1)}, bf16[2048,2048]{1,0:T(8,128)(2,1)}, f32[2048,1]{1,0:T(8,128)}, f32[32,512]{1,0:T(8,128)}) custom-call(s32[1]{0:T(128)} %bitcast.expert_ref, bf16[32,64,512]{2,1,0:T(8,128)(2,1)} %all-to-all-done.x_ref, bf16[2048,2048]{1,0:T(8,128)(2,1)} %shard_map.223.gw_ref, ...), custom_call_target="tpu_custom_call" | custom-call | flops 8589934592 | bytes 33554432 | tf_op jit(solution)/shard_map/pallas_call | solution.py:556
  117.4 9.2 %all-to-all-start.3 = ((bf16[32,64,512]{2,1,0:T(8,128)(2,1)}), bf16[32,64,512]{2,1,0:T(8,128)(2,1)S(1)}, u32[]{:S(2)}, u32[]{:S(2)}) async-start(bf16[32,64,512]{2,1,0:T(8,128)(2,1)} %get-tuple-element.33), calls=%async_computation.3 | async-start | bytes 4194304 | tf_op jit(solution)/shard_map/all_to_all | solution.py:586
  126.6 14.7 %shard_map.229 = bf16[4,2,512,512]{3,2,1,0:T(8,128)(2,1)} custom-call(bf16[32,64,512]{2,1,0:T(8,128)(2,1)} %all-to-all-done.x_ref, bf16[32,72,512]{2,1,0:T(8,128)(2,1)} %copy-done, f32[2048,1]{1,0:T(8,128)} %get-tuple-element.31.scale_ref, bf16[2048,2048]{1,0:T(8,128)(2,1)} %get-tuple-element.30.act_ref, bf16[2048,2048]{1,0:T(8,128)(2,1)} %get-tuple-element.40.dpre_ref), custom_call_target="tpu_custom_call" | custom-call | flops 8589934592 | bytes 25165824 | tf_op jit(solution)/shard_map/pallas_call | solution.py:599
  141.3 13.6 %all-to-all-done.3.dslot_ref = bf16[32,64,512]{2,1,0:T(8,128)(2,1)S(1)} async-done(((bf16[32,64,512]{2,1,0:T(8,128)(2,1)}), bf16[32,64,512]{2,1,0:T(8,128)(2,1)S(1)}, u32[]{:S(2)}, u32[]{:S(2)}) %all-to-all-start.3) | async-done | bytes 2097184 | tf_op jit(solution)/shard_map/all_to_all | solution.py:586
  156.3 16.5 %shard_map.228 = (bf16[2304,512]{1,0:T(8,128)(2,1)}, f32[512,512]{1,0:T(8,128)}) custom-call(bf16[32,64,512]{2,1,0:T(8,128)(2,1)} %copy-done.2, f32[512,128]{1,0:T(8,128)} %get-tuple-element.26.cols_ref, s32[1,512]{1,0:T(1,128)} %seg_ref.5, bf16[512,512]{1,0:T(8,128)(2,1)} %tokens_ref.3, bf16[512,512]{1,0:T(8,128)(2,1)} %cot_ref.3, ...), custom_call_target="tpu_custom_call" | custom-call | flops 3758096384 | bytes 12394496 | tf_op jit(solution)/shard_map/pallas_call | solution.py:399
  181.9 7.0 %collective-permute-done.3 = bf16[288,512]{1,0:T(8,128)(2,1)S(1)} collective-permute-done((bf16[288,512]{1,0:T(8,128)(2,1)}, bf16[288,512]{1,0:T(8,128)(2,1)S(1)}, u32[]{:S(2)}, u32[]{:S(2)}) %collective-permute-start.3) | collective-permute-done | bytes 294944 | tf_op jit(solution)/shard_map/ppermute | solution.py:440
  190.1 7.3 %collective-permute-done.1 = bf16[288,512]{1,0:T(8,128)(2,1)S(1)} collective-permute-done((bf16[288,512]{1,0:T(8,128)(2,1)S(1)}, bf16[288,512]{1,0:T(8,128)(2,1)S(1)}, u32[]{:S(2)}, u32[]{:S(2)}) %collective-permute-start.1) | collective-permute-done | bytes 294944 | tf_op jit(solution)/shard_map/ppermute | solution.py:440
  202.6 3.0 collective-permute-done.5
  211.5 3.5 %collective-permute-done.8 = bf16[72,512]{1,0:T(8,128)(2,1)S(1)} collective-permute-done((bf16[72,512]{1,0:T(8,128)(2,1)S(1)}, bf16[72,512]{1,0:T(8,128)(2,1)S(1)}, u32[]{:S(2)}, u32[]{:S(2)}) %collective-permute-start.8) | collective-permute-done | bytes 73760 | tf_op jit(solution)/shard_map/ppermute | solution.py:448
  216.8 10.5 %shard_map.226 = bf16[32,64,512]{2,1,0:T(8,128)(2,1)} custom-call(bf16[2048,2048]{1,0:T(8,128)(2,1)} %get-tuple-element.30.act_ref, bf16[4,512,512]{2,1,0:T(8,128)(2,1)} %all-gather.4.cloned.1.call-done.w2_ref, f32[2048,1]{1,0:T(8,128)} %get-tuple-element.31.scale_ref), custom_call_target="tpu_custom_call" | custom-call | flops 4294967296 | bytes 12582912 | tf_op jit(solution)/shard_map/pallas_call | solution.py:588
  227.3 7.8 %all-to-all-start.2 = ((bf16[32,64,512]{2,1,0:T(8,128)(2,1)}), bf16[32,64,512]{2,1,0:T(8,128)(2,1)S(1)}, u32[]{:S(2)}, u32[]{:S(2)}) async-start(bf16[32,64,512]{2,1,0:T(8,128)(2,1)} %shard_map.226), calls=%async_computation.2 | async-start | bytes 4194304 | tf_op jit(solution)/shard_map/all_to_all | solution.py:597
  235.1 3.0 collective-permute-start.11
  239.6 19.9 %collective-permute-done.11 = bf16[72,512]{1,0:T(8,128)(2,1)S(1)} collective-permute-done((bf16[72,512]{1,0:T(8,128)(2,1)S(1)}, bf16[72,512]{1,0:T(8,128)(2,1)S(1)}, u32[]{:S(2)}, u32[]{:S(2)}) %collective-permute-start.11) | collective-permute-done | bytes 73760 | tf_op jit(solution)/shard_map/ppermute | solution.py:457
  260.2 2.9 collective-permute-done.12
  273.4 7.4 %collective-permute-done.14 = bf16[288,512]{1,0:T(8,128)(2,1)} collective-permute-done((bf16[288,512]{1,0:T(8,128)(2,1)}, bf16[288,512]{1,0:T(8,128)(2,1)}, u32[]{:S(2)}, u32[]{:S(2)}) %collective-permute-start.14) | collective-permute-done | bytes 294944 | tf_op jit(solution)/shard_map/ppermute | solution.py:457
  285.0 4.1 %shard_map.227 = bf16[512,512]{1,0:T(8,128)(2,1)} custom-call(bf16[32,64,512]{2,1,0:T(8,128)(2,1)} %copy-done.1, f32[512,128]{1,0:T(8,128)} %get-tuple-element.26.cols_ref, f32[512,512]{1,0:T(8,128)} %get-tuple-element.32.residual_ref), custom_call_target="tpu_custom_call" | custom-call | flops 1073741824 | bytes 3932160 | tf_op jit(solution)/shard_map/pallas_call | solution.py:399
  (78 shorter events, 58.8 us)
Async XLA Ops:
  7.2 72.2 %all-gather.4.cloned.1.call-start = ((), (), s32[]{:S(2)}) async-start(), calls=%async_computation.5 | async-start | bytes 2621440 | tf_op jit(solution)/shard_map/all_gather | solution.py:488
  12.7 39.7 %all-to-all-start.1 = ((bf16[32,72,512]{2,1,0:T(8,128)(2,1)}), bf16[32,72,512]{2,1,0:T(8,128)(2,1)S(1)}, u32[]{:S(2)}, u32[]{:S(2)}) async-start(bf16[32,72,512]{2,1,0:T(8,128)(2,1)} %get-tuple-element.29), calls=%async_computation.1 | async-start | bytes 4718592 | tf_op jit(solution)/shard_map/all_to_all | solution.py:505
  21.3 68.4 %all-gather.6.cloned.1.call-start = ((), (), s32[]{:S(2)}) async-start(), calls=%async_computation.6 | async-start | bytes 2621440 | tf_op jit(solution)/shard_map/all_gather | solution.py:489
  52.5 37.2 %all-to-all-start = ((bf16[32,64,512]{2,1,0:T(8,128)(2,1)}), bf16[32,64,512]{2,1,0:T(8,128)(2,1)}, u32[]{:S(2)}, u32[]{:S(2)}) async-start(bf16[32,64,512]{2,1,0:T(8,128)(2,1)} %get-tuple-element.28), calls=%async_computation | async-start | bytes 4194304 | tf_op jit(solution)/shard_map/all_to_all | solution.py:528
  117.4 37.5 %all-to-all-start.3 = ((bf16[32,64,512]{2,1,0:T(8,128)(2,1)}), bf16[32,64,512]{2,1,0:T(8,128)(2,1)S(1)}, u32[]{:S(2)}, u32[]{:S(2)}) async-start(bf16[32,64,512]{2,1,0:T(8,128)(2,1)} %get-tuple-element.33), calls=%async_computation.3 | async-start | bytes 4194304 | tf_op jit(solution)/shard_map/all_to_all | solution.py:586
  126.6 169.5 %reduce-scatter.2.cloned.1.call-start = ((), (), s32[]{:S(2)}) async-start(), calls=%async_computation.7 | async-start | bytes 5242880 | tf_op jit(solution)/shard_map/reduce_scatter | solution.py:614
  174.1 3.7 %collective-permute-start = (bf16[1152,512]{1,0:T(8,128)(2,1)S(1)}, bf16[1152,512]{1,0:T(8,128)(2,1)S(1)}, u32[]{:S(2)}, u32[]{:S(2)}) collective-permute-start(bf16[1152,512]{1,0:T(8,128)(2,1)S(1)} %constant_dynamic-slice_fusion.6), channel_id=1, source_target_pairs={{0,1},{1,0},{2,3},{3,2},{4,5},{5,4},{6,7},{7,6},{8,9},{9,8},{10,11... | collective-permute-start | bytes 3538952 | tf_op jit(solution)/shard_map/ppermute | solution.py:434
  180.4 8.4 %collective-permute-start.3 = (bf16[288,512]{1,0:T(8,128)(2,1)}, bf16[288,512]{1,0:T(8,128)(2,1)S(1)}, u32[]{:S(2)}, u32[]{:S(2)}) collective-permute-start(bf16[288,512]{1,0:T(8,128)(2,1)} %get-tuple-element.60), channel_id=1, source_target_pairs={{0,24},{1,25},{2,26},{3,27},{4,28},{5,29},{6,30},{7,31},{8,0},{9,1... | collective-permute-start | bytes 884744 | tf_op jit(solution)/shard_map/ppermute | solution.py:440
  180.5 9.6 %collective-permute-start.2 = (bf16[288,512]{1,0:T(8,128)(2,1)}, bf16[288,512]{1,0:T(8,128)(2,1)S(1)}, u32[]{:S(2)}, u32[]{:S(2)}) collective-permute-start(bf16[288,512]{1,0:T(8,128)(2,1)} %get-tuple-element.61), channel_id=1, source_target_pairs={{0,16},{1,17},{2,18},{3,19},{4,20},{5,21},{6,22},{7,23},{8,24},{9,... | collective-permute-start | bytes 884744 | tf_op jit(solution)/shard_map/ppermute | solution.py:440
  180.8 16.6 %collective-permute-start.1 = (bf16[288,512]{1,0:T(8,128)(2,1)S(1)}, bf16[288,512]{1,0:T(8,128)(2,1)S(1)}, u32[]{:S(2)}, u32[]{:S(2)}) collective-permute-start(bf16[288,512]{1,0:T(8,128)(2,1)S(1)} %get-tuple-element.59), channel_id=1, source_target_pairs={{0,8},{1,9},{2,10},{3,11},{4,12},{5,13},{6,14},{7,15},{8,16},{9,17... | collective-permute-start | bytes 884744 | tf_op jit(solution)/shard_map/ppermute | solution.py:440
  199.3 3.3 %collective-permute-start.6 = (bf16[72,512]{1,0:T(8,128)(2,1)S(1)}, bf16[72,512]{1,0:T(8,128)(2,1)S(1)}, u32[]{:S(2)}, u32[]{:S(2)}) collective-permute-start(bf16[72,512]{1,0:T(8,128)(2,1)S(1)} %get-tuple-element.63), channel_id=1, source_target_pairs={{0,6},{1,7},{2,0},{3,1},{4,2},{5,3},{6,4},{7,5},{8,14},{9,15},{10,... | collective-permute-start | bytes 221192 | tf_op jit(solution)/shard_map/ppermute | solution.py:440
  200.8 4.8 %collective-permute-start.5 = (bf16[72,512]{1,0:T(8,128)(2,1)S(1)}, bf16[72,512]{1,0:T(8,128)(2,1)S(1)}, u32[]{:S(2)}, u32[]{:S(2)}) collective-permute-start(bf16[72,512]{1,0:T(8,128)(2,1)S(1)} %get-tuple-element.64), channel_id=1, source_target_pairs={{0,4},{1,5},{2,6},{3,7},{4,0},{5,1},{6,2},{7,3},{8,12},{9,13},{10,... | collective-permute-start | bytes 221192 | tf_op jit(solution)/shard_map/ppermute | solution.py:440
  201.0 6.4 %collective-permute-start.4 = (bf16[72,512]{1,0:T(8,128)(2,1)S(1)}, bf16[72,512]{1,0:T(8,128)(2,1)S(1)}, u32[]{:S(2)}, u32[]{:S(2)}) collective-permute-start(bf16[72,512]{1,0:T(8,128)(2,1)S(1)} %get-tuple-element.62), channel_id=1, source_target_pairs={{0,2},{1,3},{2,4},{3,5},{4,6},{5,7},{6,0},{7,1},{8,10},{9,11},{10,... | collective-permute-start | bytes 221192 | tf_op jit(solution)/shard_map/ppermute | solution.py:440
  207.5 4.1 %collective-permute-start.9 = (bf16[72,512]{1,0:T(8,128)(2,1)S(1)}, bf16[72,512]{1,0:T(8,128)(2,1)S(1)}, u32[]{:S(2)}, u32[]{:S(2)}) collective-permute-start(bf16[72,512]{1,0:T(8,128)(2,1)S(1)} %add_convert_fusion.1), channel_id=1, source_target_pairs={{0,96},{32,0},{64,32},{96,64},{1,97},{33,1},{65,33},{97,65},{2,98}... | collective-permute-start | bytes 221192 | tf_op jit(solution)/shard_map/ppermute | solution.py:448
  210.1 4.9 %collective-permute-start.8 = (bf16[72,512]{1,0:T(8,128)(2,1)S(1)}, bf16[72,512]{1,0:T(8,128)(2,1)S(1)}, u32[]{:S(2)}, u32[]{:S(2)}) collective-permute-start(bf16[72,512]{1,0:T(8,128)(2,1)S(1)} %add_convert_fusion.1), channel_id=1, source_target_pairs={{0,32},{32,64},{64,96},{96,0},{1,33},{33,65},{65,97},{97,1},{2,34}... | collective-permute-start | bytes 221192 | tf_op jit(solution)/shard_map/ppermute | solution.py:448
  210.1 5.3 %collective-permute-start.7 = (bf16[72,512]{1,0:T(8,128)(2,1)S(1)}, bf16[72,512]{1,0:T(8,128)(2,1)S(1)}, u32[]{:S(2)}, u32[]{:S(2)}) collective-permute-start(bf16[72,512]{1,0:T(8,128)(2,1)S(1)} %add_convert_fusion.1), channel_id=1, source_target_pairs={{0,64},{32,96},{64,0},{96,32},{1,65},{33,97},{65,1},{97,33},{2,66}... | collective-permute-start | bytes 221192 | tf_op jit(solution)/shard_map/ppermute | solution.py:448
  216.8 22.2 %collective-permute-start.10 = (bf16[72,512]{1,0:T(8,128)(2,1)S(1)}, bf16[72,512]{1,0:T(8,128)(2,1)S(1)}, u32[]{:S(2)}, u32[]{:S(2)}) collective-permute-start(bf16[72,512]{1,0:T(8,128)(2,1)S(1)} %get-tuple-element.42), channel_id=1, source_target_pairs={{0,2},{1,3},{2,4},{3,5},{4,6},{5,7},{6,0},{7,1},{8,10},{9,11},{10,... | collective-permute-start | bytes 221192 | tf_op jit(solution)/shard_map/ppermute | solution.py:457
  227.3 56.4 %all-to-all-start.2 = ((bf16[32,64,512]{2,1,0:T(8,128)(2,1)}), bf16[32,64,512]{2,1,0:T(8,128)(2,1)S(1)}, u32[]{:S(2)}, u32[]{:S(2)}) async-start(bf16[32,64,512]{2,1,0:T(8,128)(2,1)} %shard_map.226), calls=%async_computation.2 | async-start | bytes 4194304 | tf_op jit(solution)/shard_map/all_to_all | solution.py:597
  235.1 24.4 %collective-permute-start.11 = (bf16[72,512]{1,0:T(8,128)(2,1)S(1)}, bf16[72,512]{1,0:T(8,128)(2,1)S(1)}, u32[]{:S(2)}, u32[]{:S(2)}) collective-permute-start(bf16[72,512]{1,0:T(8,128)(2,1)S(1)} %get-tuple-element.42), channel_id=1, source_target_pairs={{0,4},{1,5},{2,6},{3,7},{4,0},{5,1},{6,2},{7,3},{8,12},{9,13},{10,... | collective-permute-start | bytes 221192 | tf_op jit(solution)/shard_map/ppermute | solution.py:457
  238.1 25.0 %collective-permute-start.12 = (bf16[72,512]{1,0:T(8,128)(2,1)S(1)}, bf16[72,512]{1,0:T(8,128)(2,1)S(1)}, u32[]{:S(2)}, u32[]{:S(2)}) collective-permute-start(bf16[72,512]{1,0:T(8,128)(2,1)S(1)} %get-tuple-element.42), channel_id=1, source_target_pairs={{0,6},{1,7},{2,0},{3,1},{4,2},{5,3},{6,4},{7,5},{8,14},{9,15},{10,... | collective-permute-start | bytes 221192 | tf_op jit(solution)/shard_map/ppermute | solution.py:457
  263.8 8.6 %collective-permute-start.13 = (bf16[288,512]{1,0:T(8,128)(2,1)}, bf16[288,512]{1,0:T(8,128)(2,1)}, u32[]{:S(2)}, u32[]{:S(2)}) collective-permute-start(bf16[288,512]{1,0:T(8,128)(2,1)} %constant_dynamic-update-slice_fusion.4), channel_id=1, source_target_pairs={{0,8},{1,9},{2,10},{3,11},{4,12},{5,13},{6,14},{7,15},{8,16},{9,17... | collective-permute-start | bytes 884744 | tf_op jit(solution)/shard_map/ppermute | solution.py:457
  265.6 15.2 %collective-permute-start.14 = (bf16[288,512]{1,0:T(8,128)(2,1)}, bf16[288,512]{1,0:T(8,128)(2,1)}, u32[]{:S(2)}, u32[]{:S(2)}) collective-permute-start(bf16[288,512]{1,0:T(8,128)(2,1)} %constant_dynamic-update-slice_fusion.4), channel_id=1, source_target_pairs={{0,16},{1,17},{2,18},{3,19},{4,20},{5,21},{6,22},{7,23},{8,24},{9,... | collective-permute-start | bytes 884744 | tf_op jit(solution)/shard_map/ppermute | solution.py:457
  268.0 13.8 %collective-permute-start.15 = (bf16[288,512]{1,0:T(8,128)(2,1)}, bf16[288,512]{1,0:T(8,128)(2,1)S(1)}, u32[]{:S(2)}, u32[]{:S(2)}) collective-permute-start(bf16[288,512]{1,0:T(8,128)(2,1)} %constant_dynamic-update-slice_fusion.4), channel_id=1, source_target_pairs={{0,24},{1,25},{2,26},{3,27},{4,28},{5,29},{6,30},{7,31},{8,0},{9,1... | collective-permute-start | bytes 884744 | tf_op jit(solution)/shard_map/ppermute | solution.py:457
  281.8 7.3 %collective-permute-start.16 = (bf16[1152,512]{1,0:T(8,128)(2,1)S(1)}, bf16[1152,512]{1,0:T(8,128)(2,1)}, u32[]{:S(2)}, u32[]{:S(2)}) collective-permute-start(bf16[1152,512]{1,0:T(8,128)(2,1)S(1)} %constant_dynamic-update-slice_fusion), channel_id=1, source_target_pairs={{0,1},{1,0},{2,3},{3,2},{4,5},{5,4},{6,7},{7,6},{8,9},{9,8},{10,11... | collective-permute-start | bytes 3538952 | tf_op jit(solution)/shard_map/ppermute | solution.py:462
  (5 other events, 50.4 us)
Sparse Core Ops, SparseCore 0:
  9.7 34.2 all-gather.3
  45.6 31.4 all-gather.5
  141.4 47.8 reduce-scatter.1
